TPU v7x, 32 devices: a whole 2x2x4 slice. The times are simulated.
32 devices in a mesh: vocab: 16 (over z, y, core), width: 2 (over x).
Axes of the slice: x: 2, y: 2, z: 4, core: 2. Of those that a mesh axis runs over, the one named last changes fastest.
Arguments:
- hidden: bfloat16 [128, 4608], P('vocab', 'width'), may hold values from -72 to 72
- pre_gain: float32 [4608], P('width'), may hold values from 0.1 to 1.9
- post_gain: float32 [4608], P('width'), may hold values from 0.1 to 1.9
- final_gain: float32 [4608], P('width'), may hold values from 0.1 to 1.9
- gate_weight: bfloat16 [4608, 18432], P('width', 'vocab'), may hold values from -0.09375 to 0.09375
- up_weight: bfloat16 [4608, 18432], P('width', 'vocab'), may hold values from -0.09375 to 0.09375
- down_weight: bfloat16 [18432, 4608], P('vocab', 'width'), may hold values from -2 to 2
- head_weight: bfloat16 [4608, 65536], P('width', 'vocab'), may hold values from -0.25 to 0.25
- token_ids: int32 [128], replicated, may hold values from 0 to 65535
- rewards: float32 [16], replicated, may hold values from -3 to 3
Outputs:
- grad_hidden: bfloat16 [128, 4608], P('vocab', 'width')
- grad_gate: bfloat16 [4608, 18432], P('width', 'vocab')
- grad_up: bfloat16 [4608, 18432], P('width', 'vocab')
- grad_down: bfloat16 [18432, 4608], P('vocab', 'width')
- grad_head: bfloat16 [4608, 65536], P('width', 'vocab')
- loss: float32 [], replicated
All inputs are finite; a program needn't handle non-finite values.
Results may differ from a plain program's by a relative error of at most 0.013.
Values may be sent and summed in bfloat16 or wider, within the bound.
A program may use at most 128 MiB of HBM per device.

v0:
```python
import math

import jax
import jax.numpy as jnp
from jax import lax
from jax.sharding import PartitionSpec as P

CAP = 30


EPS = 1e-06
ROOT_TWO_PI = math.sqrt(2.0 / math.pi)


def gelu_value(value):
    inner = ROOT_TWO_PI * (value + 0.044715 * value * value * value)
    return 0.5 * value * (1.0 + jnp.tanh(inner))


def gelu_slope(value):
    bent = jnp.tanh(ROOT_TWO_PI * (value + 0.044715 * value * value * value))
    return 0.5 * (1.0 + bent) + 0.5 * value * (1.0 - bent * bent) * ROOT_TWO_PI * (
        1.0 + 3.0 * 0.044715 * value * value
    )


def contract(left, right, left_dim, right_dim):
    return lax.dot_general(
        left, right, (((left_dim,), (right_dim,)), ((), ())), preferred_element_type=jnp.float32
    )


def shards(
    hidden,
    pre_gain,
    post_gain,
    final_gain,
    gate_weight,
    up_weight,
    down_weight,
    head_weight,
    token_ids,
    rewards,
):
    tok_dev = hidden.shape[0]
    width_dev = hidden.shape[1]
    model = width_dev * lax.axis_size("width")
    vocab_index = lax.axis_index("vocab")
    width_index = lax.axis_index("width")
    own_start = vocab_index * tok_dev
    gathered = lax.all_gather(hidden, "vocab", axis=0, tiled=True)
    inputs = gathered.astype(jnp.float32)
    squares_pre = lax.psum(jnp.sum(inputs * inputs, axis=1), "width")
    scale_pre = lax.rsqrt(squares_pre / model + EPS)[:, None]
    normed = (inputs * scale_pre * pre_gain).astype(jnp.bfloat16)
    gate_part = jnp.dot(normed, gate_weight, preferred_element_type=jnp.float32)
    upward_part = jnp.dot(normed, up_weight, preferred_element_type=jnp.float32)
    gate, upward = lax.psum((gate_part, upward_part), "width")
    gelu_gate = gelu_value(gate)
    active = (gelu_gate * upward).astype(jnp.bfloat16)
    branch = lax.psum(jnp.dot(active, down_weight, preferred_element_type=jnp.float32), "vocab")
    branch_gain = branch * post_gain
    squares_post = lax.psum(jnp.sum(branch * branch, axis=1), "width")
    scale_post = lax.rsqrt(squares_post / model + EPS)[:, None]
    resid = inputs + scale_post * branch_gain
    squares_final = lax.psum(jnp.sum(resid * resid, axis=1), "width")
    scale_final = lax.rsqrt(squares_final / model + EPS)[:, None]
    final = (resid * scale_final * final_gain).astype(jnp.bfloat16)
    vocab_dev = head_weight.shape[1]
    sub_rows = vocab_dev // lax.axis_size("width")
    columns = head_weight
    logits = lax.psum_scatter(
        contract(columns, final, 0, 1), "width", scatter_dimension=0, tiled=True
    )
    capped = CAP * jnp.tanh(logits / CAP)
    first_column = vocab_index * vocab_dev + width_index * sub_rows
    column_ids = first_column + jnp.arange(sub_rows, dtype=jnp.int32)
    hits = column_ids[:, None] == token_ids[None, :]
    total, target = lax.psum(
        (jnp.sum(jnp.exp(capped - CAP), axis=0), jnp.sum(jnp.where(hits, capped, 0.0), axis=0)),
        ("vocab", "width"),
    )
    lognorm = CAP + jnp.log(total)
    logprob = target - lognorm
    weights = jnp.repeat(rewards, token_ids.shape[0] // rewards.shape[0])
    loss = -jnp.mean(weights * logprob)
    prob = jnp.exp(capped - lognorm[None, :])
    slope = 1.0 - (capped / CAP) ** 2
    delta = (-weights[None, :] * (hits.astype(jnp.float32) - prob) * slope).astype(jnp.bfloat16)
    piece = lax.all_gather(delta, "width", axis=0, tiled=True)
    columns = head_weight
    block = contract(final, piece, 0, 1)
    grad_cols = block
    grad_rows = contract(piece, columns, 0, 1)
    grad_cols, grad_rows = (grad_cols, grad_rows)
    grad_head = grad_cols.astype(jnp.bfloat16)
    grad_final = lax.psum(grad_rows, "vocab")
    weighted = grad_final * final_gain
    back_final = lax.psum(jnp.sum(weighted * resid, axis=1), "width")[:, None]
    grad_resid = scale_final * weighted - resid * scale_final**3 * back_final / model
    weighted_post = grad_resid * post_gain
    back_post = lax.psum(jnp.sum(weighted_post * branch, axis=1), "width")[:, None]
    grad_branch = (
        scale_post * weighted_post - branch * scale_post**3 * back_post / model
    ).astype(jnp.bfloat16)
    resid_rows = lax.dynamic_slice_in_dim(grad_resid, own_start, tok_dev, 0)
    grad_down = contract(active, grad_branch, 0, 0).astype(jnp.bfloat16)
    grad_active = lax.psum(contract(grad_branch, down_weight, 1, 1), "width")
    grad_gate_in = (grad_active * upward * gelu_slope(gate)).astype(jnp.bfloat16)
    grad_up_in = (grad_active * gelu_gate).astype(jnp.bfloat16)
    grad_gate = contract(normed, grad_gate_in, 0, 0).astype(jnp.bfloat16)
    grad_up = contract(normed, grad_up_in, 0, 0).astype(jnp.bfloat16)
    grad_normed = lax.psum_scatter(
        contract(grad_gate_in, gate_weight, 1, 1) + contract(grad_up_in, up_weight, 1, 1),
        "vocab",
        scatter_dimension=0,
        tiled=True,
    )
    own_inputs = hidden.astype(jnp.float32)
    own_scale = lax.dynamic_slice_in_dim(scale_pre, own_start, tok_dev, 0)
    weighted_pre = grad_normed * pre_gain
    back_pre = lax.psum(jnp.sum(weighted_pre * own_inputs, axis=1), "width")[:, None]
    grad_hidden = (
        resid_rows + own_scale * weighted_pre - own_inputs * own_scale**3 * back_pre / model
    ).astype(jnp.bfloat16)
    return (grad_hidden, grad_gate, grad_up, grad_down, grad_head, loss)


def solution(mesh):
    return jax.shard_map(
        shards,
        mesh=mesh,
        in_specs=(
            P("vocab", "width"),
            P("width"),
            P("width"),
            P("width"),
            P("width", "vocab"),
            P("width", "vocab"),
            P("vocab", "width"),
            P("width", "vocab"),
            P(),
            P(),
        ),
        out_specs=(
            P("vocab", "width"),
            P("width", "vocab"),
            P("width", "vocab"),
            P("vocab", "width"),
            P("width", "vocab"),
            P(),
        ),
        check_vma=False,
    )
```

profile of v0, /device:TPU:0, one launch (start us, length us, event | category | flops | bytes accessed | tf_op | source)
XLA Modules:
  0.0 551.8 jit_solution(17728710412057641691)
XLA Ops:
  7.2 25.1 %all_gather.6 = bf16[128,2304]{1,0:T(8,128)(2,1)S(1)} all-gather(bf16[8,2304]{1,0:T(8,128)(2,1)} %param.10), channel_id=1, replica_groups=mesh['vocab'=16,'width'=2] {'vocab'}, dimensions={0}, use_global_device_ids=true | all-gather | bytes 626688 | tf_op jit(solution)/shard_map/all_gather | solution.py:51
  32.5 4.9 psum.91
  37.4 4.5 fusion.23
  41.9 1.8 fusion.25
  43.8 40.5 %all-reduce.13.cloned.1.call-done = (f32[128,1152]{1,0:T(8,128)}, f32[128,1152]{1,0:T(8,128)}) async-done(((f32[128,1152]{1,0:T(8,128)}, f32[128,1152]{1,0:T(8,128)}), (f32[128,1152]{1,0:T(8,128)}, f32[128,1152]{1,0:T(8,128)})) %all-reduce.13.cloned.1.call-update) | async-done | bytes 1179664 | tf_op jit(solution)/shard_map/psum | solution.py:58
  85.7 4.6 fusion.27
  90.4 93.9 %all-reduce.7.cloned.1.call-done = f32[128,2304]{1,0:T(8,128)} async-done(((f32[128,2304]{1,0:T(8,128)}), f32[128,2304]{1,0:T(8,128)}) %all-reduce.7.cloned.1.call-update) | async-done | bytes 1179664 | tf_op jit(solution)/shard_map/psum | solution.py:61
  185.8 4.9 psum.95
  191.8 4.9 psum.96
  196.8 10.4 %convolution_bitcast_fusion = f32[4096,128]{0,1:T(8,128)} fusion(bf16[2304,4096]{1,0:T(8,128)(2,1)} %param.17, f32[128,2304]{1,0:T(8,128)S(1)} %get-tuple-element.17, f32[2304]{0:T(1024)S(1)} %copy-done.13, f32[128]{0:T(128)S(1)} %get-tuple-element.26), kind=kOutput, calls=%fused_computation.4 | convolution fusion | flops 2416803840 | bytes 22160896 | tf_op jit(solution)/shard_map/dot_general | solution.py:28
  208.0 30.1 %reduce-scatter.3.cloned.1.call-done = f32[2048,128]{0,1:T(8,128)} async-done(((f32[4096,128]{0,1:T(8,128)}), f32[2048,128]{0,1:T(8,128)}) %reduce-scatter.3.cloned.1.call-update) | async-done | bytes 1048592 | tf_op jit(solution)/shard_map/reduce_scatter | solution.py:72
  238.1 1.8 fusion.7
  239.8 39.4 %all-reduce = (f32[128]{0:T(128)S(1)}, f32[128]{0:T(128)S(1)}) all-reduce(f32[128]{0:T(128)S(1)} %get-tuple-element.7, f32[128]{0:T(128)S(1)} %get-tuple-element.6), channel_id=1, replica_groups=mesh['vocab'=16,'width'=2] {'vocab','width'}, use_global_device_ids=true, to_apply=%region_11.12 | all-reduce | flops 256 | bytes 2048 | tf_op jit(solution)/shard_map/psum | solution.py:79
  279.8 2.6 fusion.6
  282.6 22.0 %all-gather.2.cloned.1.call-done = bf16[4096,128]{0,1:T(8,128)(2,1)} async-done(((bf16[2048,128]{0,1:T(8,128)(2,1)}), bf16[4096,128]{0,1:T(8,128)(2,1)}) %all-gather.2.cloned.1.call-update) | async-done | bytes 1048592 | tf_op jit(solution)/shard_map/all_gather | solution.py:90
  304.6 14.1 %fusion.28 = f32[128,2304]{1,0:T(8,128)} fusion(bf16[4096,128]{0,1:T(8,128)(2,1)} %all-gather.2.cloned.1.call-done, bf16[2304,4096]{1,0:T(8,128)(2,1)} %param.17), kind=kOutput, calls=%fused_computation.60 | convolution fusion | flops 2415919104 | bytes 21102592 | tf_op jit(solution)/shard_map/dot_general | solution.py:28
  318.7 93.8 %all-reduce.9.cloned.1.call-done = f32[128,2304]{1,0:T(8,128)} async-done(((f32[128,2304]{1,0:T(8,128)}), f32[128,2304]{1,0:T(8,128)}) %all-reduce.9.cloned.1.call-update) | async-done | bytes 1179664 | tf_op jit(solution)/shard_map/psum | solution.py:97
  414.0 4.9 psum.99
  419.0 2.7 multiply_reduce_fusion
  421.7 5.4 psum.100
  427.1 1.7 subtract_convert_fusion
  428.8 5.2 fusion.29
  435.5 27.6 %all-reduce.11.cloned.1.call-done = f32[128,1152]{1,0:T(8,128)} async-done(((f32[128,1152]{1,0:T(8,128)}), f32[128,1152]{1,0:T(8,128)}) %all-reduce.11.cloned.1.call-update) | async-done | bytes 589840 | tf_op jit(solution)/shard_map/psum | solution.py:108
  464.6 4.3 fusion.30
  468.9 5.1 convolution_add_fusion
  475.2 9.6 %convolution_convert_fusion = bf16[2304,4096]{1,0:T(8,128)(2,1)} fusion(bf16[4096,128]{0,1:T(8,128)(2,1)S(1)} %copy-done.2, f32[128,2304]{1,0:T(8,128)S(1)} %get-tuple-element.17, f32[2304]{0:T(1024)S(1)} %copy-done.14, f32[128]{0:T(128)S(1)} %copy-done.18), kind=kOutput, calls=%fused_computation | convolution fusion | flops 2426241024 | bytes 21112320 | tf_op jit(solution)/shard_map/dot_general | solution.py:28
  484.8 4.0 convolution_convert_fusion.1
  488.8 4.0 convolution_convert_fusion.2
  492.8 39.4 %reduce-scatter.5.cloned.1.call-done = f32[8,2304]{1,0:T(8,128)} async-done(((f32[128,2304]{1,0:T(8,128)}), f32[8,2304]{1,0:T(8,128)}) %reduce-scatter.5.cloned.1.call-update) | async-done | bytes 73744 | tf_op jit(solution)/shard_map/reduce_scatter | solution.py:113
  533.2 4.0 convolution_convert_fusion.3
  537.3 4.9 psum.102
  542.2 1.6 fusion.19
  (77 shorter events, 12.3 us)
Async XLA Ops:
  7.2 30.3 %copy-start.11 = (f32[2304]{0:T(1024)S(1)}, f32[2304]{0:T(1024)}, u32[]{:S(2)}) copy-start(f32[2304]{0:T(1024)} %param.11) | copy-start | bytes 27652
  7.2 77.1 %all-reduce.13.cloned.1.call-start = ((), (), s32[]{:S(2)}) async-start(), calls=%async_computation.8 | async-start | bytes 2359296 | tf_op jit(solution)/shard_map/psum | solution.py:58
  37.4 4.5 copy-start
  43.7 140.5 %all-reduce.7.cloned.1.call-start = ((), (), s32[]{:S(2)}) async-start(), calls=%async_computation.2 | async-start | bytes 2359296 | tf_op jit(solution)/shard_map/psum | solution.py:61
  85.7 4.6 copy-start.3
  90.3 101.0 %copy-start.16 = (f32[2304]{0:T(1024)S(1)}, f32[2304]{0:T(1024)}, u32[]{:S(2)}) copy-start(f32[2304]{0:T(1024)} %param.12) | copy-start | bytes 27652
  90.3 147.7 %reduce-scatter.3.cloned.1.call-start = ((), (), s32[]{:S(2)}) async-start(), calls=%async_computation.3 | async-start | bytes 3145728 | tf_op jit(solution)/shard_map/reduce_scatter | solution.py:72
  184.3 7.0 %copy-start.1 = (f32[128,2304]{1,0:T(8,128)S(1)}, f32[128,2304]{1,0:T(8,128)}, u32[]{:S(2)}) copy-start(f32[128,2304]{1,0:T(8,128)} %all-reduce.7.cloned.1.call-done) | copy-start | bytes 3538948
  191.3 0.5 copy-start.22
  191.3 5.5 copy-start.13
  196.7 222.2 %copy-start.17 = (f32[128]{0:T(128)}, f32[128]{0:T(128)S(1)}, u32[]{:S(2)}) copy-start(f32[128]{0:T(128)S(1)} %get-tuple-element.26) | copy-start | bytes 1540
  207.1 0.7 copy-start.23
  207.1 30.9 %copy-start.19 = (s32[128]{0:T(128)S(1)}, s32[128]{0:T(128)}, u32[]{:S(2)}) copy-start(s32[128]{0:T(128)} %param.18) | copy-start | bytes 1540
  207.2 97.5 %all-gather.2.cloned.1.call-start = ((), (), s32[]{:S(2)}) async-start(), calls=%async_computation.4 | async-start | bytes 1572864 | tf_op jit(solution)/shard_map/all_gather | solution.py:90
  282.4 130.1 %all-reduce.9.cloned.1.call-start = ((), (), s32[]{:S(2)}) async-start(), calls=%async_computation.5 | async-start | bytes 2359296 | tf_op jit(solution)/shard_map/psum | solution.py:97
  318.7 144.4 %all-reduce.11.cloned.1.call-start = ((), (), s32[]{:S(2)}) async-start(), calls=%async_computation.6 | async-start | bytes 1179648 | tf_op jit(solution)/shard_map/psum | solution.py:108
  428.8 34.3 %copy-start.9 = (f32[128,1152]{1,0:T(8,128)S(1)}, f32[128,1152]{1,0:T(8,128)}, u32[]{:S(2)}) copy-start(f32[128,1152]{1,0:T(8,128)} %get-tuple-element.10) | copy-start | bytes 1769476
  428.8 34.3 %copy-start.10 = (f32[128,1152]{1,0:T(8,128)S(1)}, f32[128,1152]{1,0:T(8,128)}, u32[]{:S(2)}) copy-start(f32[128,1152]{1,0:T(8,128)} %get-tuple-element.11) | copy-start | bytes 1769476
  434.0 98.2 %reduce-scatter.5.cloned.1.call-start = ((), (), s32[]{:S(2)}) async-start(), calls=%async_computation.7 | async-start | bytes 1253376 | tf_op jit(solution)/shard_map/reduce_scatter | solution.py:113
  464.6 4.3 copy-start.5
  464.6 4.3 copy-start.7
  474.0 1.2 copy-start.2
  474.0 1.2 copy-start.14
  474.0 1.2 copy-start.18
  475.2 9.6 %copy-start.4 = (bf16[128,1152]{1,0:T(8,128)(2,1)S(1)}, bf16[128,1152]{1,0:T(8,128)(2,1)}, u32[]{:S(2)}) copy-start(bf16[128,1152]{1,0:T(8,128)(2,1)} %copy-done.3) | copy-start | bytes 884740
  484.8 4.0 copy-start.8
  488.8 43.4 %copy-start.12 = (bf16[8,2304]{1,0:T(8,128)(2,1)S(1)}, bf16[8,2304]{1,0:T(8,128)(2,1)}, u32[]{:S(2)}) copy-start(bf16[8,2304]{1,0:T(8,128)(2,1)} %param.10) | copy-start | bytes 110596
  488.8 44.4 %copy-start.6 = (bf16[128,1152]{1,0:T(8,128)(2,1)S(1)}, bf16[128,1152]{1,0:T(8,128)(2,1)}, u32[]{:S(2)}) copy-start(bf16[128,1152]{1,0:T(8,128)(2,1)} %copy-done.5) | copy-start | bytes 884740
  533.2 9.0 %copy-start.15 = (f32[8,2304]{1,0:T(8,128)S(1)}, f32[8,2304]{1,0:T(8,128)}, u32[]{:S(2)}) copy-start(f32[8,2304]{1,0:T(8,128)} %reduce-scatter.5.cloned.1.call-done) | copy-start | bytes 221188
  533.2 9.0 %copy-start.20 = (f32[8]{0:T(128)S(1)}, f32[8]{0:T(128)}, u32[]{:S(2)}) copy-start(f32[8]{0:T(128)} %get-tuple-element.12) | copy-start | bytes 100
  533.2 9.0 %copy-start.21 = (f32[8]{0:T(128)S(1)}, f32[8]{0:T(128)}, u32[]{:S(2)}) copy-start(f32[8]{0:T(128)} %get-tuple-element.13) | copy-start | bytes 100
Sparse Core Ops, SparseCore 0:
  43.9 40.3 all-reduce.12
  90.4 93.8 all-reduce.6
  207.3 30.7 reduce-scatter.2
  282.5 22.0 all-gather.1
  318.8 93.7 all-reduce.8
  434.1 28.9 all-reduce.10
  474.2 57.9 reduce-scatter.4
where the time goes:
time: 553 us; the launch traced here: 552 us
  waiting for transfers between devices  347 us (63%)
  blocking collectives  94.5 us (17%)
  matrix products  71.4 us (13%)
  other arithmetic  19.6 us (4%)
  between operations  16.1 us (3%)
    psum x1, waiting for transfers between devices, shards(): lax.psum(jnp.dot(active, down_weight, preferred_element_type=jnp.float32)...  93.9 us
    psum x1, waiting for transfers between devices, shards(): grad_final = lax.psum(grad_rows, 'vocab')  93.8 us
    dot_general x9, matrix products, contract(): lax.dot_general(left, right, (((left_dim,), (right_dim,)), ((), ())), pre...  60.6 us
    psum x1, waiting for transfers between devices, shards(): gate, upward = lax.psum((gate_part, upward_part), 'width')  40.5 us
    psum x1, blocking collectives, shards(): lax.psum((jnp.sum(jnp.exp(capped - CAP), axis=0), jnp.sum(jnp.where(hits,...  39.4 us
    reduce_scatter x1, waiting for transfers between devices, shards(): lax.psum_scatter(contract(grad_gate_in, gate_weight, 1, 1) + contract(gra...  39.4 us
    reduce_scatter x1, waiting for transfers between devices, shards(): lax.psum_scatter(contract(columns, final, 0, 1), 'width', scatter_dimensi...  30.1 us
    psum x1, waiting for transfers between devices, shards(): grad_active = lax.psum(contract(grad_branch, down_weight, 1, 1), 'width')  27.6 us
  transfers between devices with their start and end apart: 7, of which 7 were waited for; matrix products, arithmetic and copies ran while one was open for 3% of the time, Pallas kernels for 0%

commit v1 on v0

v1 whole, which is shorter than its diff:
```python
import functools
import math

import jax
import jax.numpy as jnp
from jax import lax
from jax.experimental import pallas as pl
from jax.experimental.pallas import tpu as pltpu
from jax.sharding import PartitionSpec as P

CAP = 30
EPS = 1e-06
ROOT_TWO_PI = math.sqrt(2.0 / math.pi)
MESH = pl.DeviceIdType.MESH
F32 = jnp.float32
BF16 = jnp.bfloat16
DMA = pltpu.SemaphoreType.DMA
LIMIT = 48 * 1024 * 1024


def contract(left, right, left_dim, right_dim):
    return lax.dot_general(
        left, right, (((left_dim,), (right_dim,)), ((), ())), preferred_element_type=F32
    )


def place():
    return lax.axis_index("vocab"), lax.axis_index("width")


def greet(devices):
    barrier = pltpu.get_barrier_semaphore()
    for device in devices:
        pl.semaphore_signal(barrier, inc=1, device_id=device, device_id_type=MESH)
    pl.semaphore_wait(barrier, len(devices))


def remote(src, dst, send_sem, recv_sem, device):
    return pltpu.make_async_remote_copy(
        src_ref=src,
        dst_ref=dst,
        send_sem=send_sem,
        recv_sem=recv_sem,
        device_id=device,
        device_id_type=MESH,
    )


def row_peers(nw):
    v, w = place()
    return [(v, lax.rem(w + k, nw)) for k in range(1, nw)]


def column_peers(nv):
    v, w = place()
    chips = nv // 2
    chip, core = v // 2, lax.rem(v, 2)
    same = [(lax.rem(chip + k, chips) * 2 + core, w) for k in range(1, chips)]
    return [(chip * 2 + 1 - core, w)] + same


def row_sum(value, slots, send, recv, nw):
    v, w = place()
    slots[w] = jnp.broadcast_to(value, slots.shape[1:])
    copies = []
    for k in range(1, nw):
        copy = remote(slots.at[w], slots.at[w], send.at[k], recv.at[k], (v, lax.rem(w + k, nw)))
        copy.start()
        copies.append(copy)
    for copy in copies:
        copy.wait()
    return jnp.sum(slots[...], axis=0)[:, :1]


def gather_rows(out, send, recv, near_send, near_recv, nv):
    v, w = place()
    chips = nv // 2
    chip, core = v // 2, lax.rem(v, 2)
    sibling = (chip * 2 + 1 - core, w)
    far, near = [], []
    for k in range(1, chips):
        target = (lax.rem(chip + k, chips) * 2 + core, w)
        copy = remote(out.at[v], out.at[v], send.at[k], recv.at[k], target)
        copy.start()
        far.append(copy)
    copy = remote(out.at[v], out.at[v], near_send.at[0], near_recv.at[0], sibling)
    copy.start()
    near.append(copy)
    for k in range(1, chips):
        source = lax.rem(chip + chips - k, chips) * 2 + core
        far[k - 1].wait_recv()
        copy = remote(out.at[source], out.at[source], near_send.at[k], near_recv.at[k], sibling)
        copy.start()
        near.append(copy)
    for copy in near:
        copy.wait_recv()
    for copy in far + near:
        copy.wait_send()


def scatter_sum(part, paired, stage, land, send, recv, near_send, near_recv, nv):
    v, w = place()
    chips = nv // 2
    chip, core = v // 2, lax.rem(v, 2)
    sibling = (chip * 2 + 1 - core, w)
    near, far = [None] * chips, []
    order = list(range(1, chips)) + [0]
    for k in order:
        to_chip = lax.rem(chip + k, chips)
        copy = remote(
            part.at[to_chip, 1 - core], paired.at[k], near_send.at[k], near_recv.at[k], sibling
        )
        copy.start()
        near[k] = copy
    total = None
    for k in order:
        to_chip = lax.rem(chip + k, chips)
        near[k].wait_recv()
        both = part[to_chip, core].astype(F32) + paired[k].astype(F32)
        if k == 0:
            total = both
        else:
            stage[k] = both.astype(BF16)
            copy = remote(stage.at[k], land.at[k], send.at[k], recv.at[k], (to_chip * 2 + core, w))
            copy.start()
            far.append(copy)
    for k in range(1, chips):
        far[k - 1].wait_recv()
        total = total + land[k].astype(F32)
    for copy in near + far:
        copy.wait_send()
    return total


def pre_kernel(nv, nw, model, hidden, gain, normed, scale, slots, ss, sr, gs, gr, hs, hr):
    v, _ = place()
    greet(column_peers(nv) + row_peers(nw))
    inputs = hidden[...].astype(F32)
    squares = row_sum(jnp.sum(inputs * inputs, axis=1, keepdims=True), slots, ss, sr, nw)
    factor = lax.rsqrt(squares / model + EPS)
    scale[...] = jnp.broadcast_to(factor, scale.shape)
    normed[v] = (inputs * factor * gain[...]).astype(BF16)
    gather_rows(normed, gs, gr, hs, hr, nv)


def gate_kernel(nw, gate_part, up_part, active, value, slope, mine, land, send, recv):
    v, w = place()
    greet(row_peers(nw))
    copies = []
    for half, part in enumerate((gate_part, up_part)):
        mine[half] = part[...].astype(BF16)
        for k in range(1, nw):
            copy = remote(
                mine.at[half],
                land.at[k - 1, half],
                send.at[k, half],
                recv.at[k, half],
                (v, lax.rem(w + k, nw)),
            )
            copy.start()
            copies.append(copy)
    gate, upward = gate_part[...], up_part[...]
    for copy in copies:
        copy.wait()
    for k in range(nw - 1):
        gate = gate + land[k, 0].astype(F32)
        upward = upward + land[k, 1].astype(F32)
    bent = jnp.tanh(ROOT_TWO_PI * (gate + 0.044715 * gate * gate * gate))
    gelu = 0.5 * gate * (1.0 + bent)
    active[...] = (gelu * upward).astype(BF16)
    value[...] = gelu
    slope[...] = upward * (
        0.5 * (1.0 + bent)
        + 0.5 * gate * (1.0 - bent * bent) * ROOT_TWO_PI * (1.0 + 3.0 * 0.044715 * gate * gate)
    )


def post_kernel(
    nv, nw, model,
    part, hidden, post_gain, final_gain,
    final, branch_out, resid_out, scales,
    paired, stage, land, slots, slots_two,
    ss, sr, ts, tr, gs, gr, hs, hr, ps, pr, qs, qr,
):
    v, _ = place()
    greet(column_peers(nv) + row_peers(nw))
    branch = scatter_sum(part, paired, stage, land, ps, pr, qs, qr, nv)
    squares = row_sum(jnp.sum(branch * branch, axis=1, keepdims=True), slots, ss, sr, nw)
    scale_post = lax.rsqrt(squares / model + EPS)
    resid = hidden[...].astype(F32) + branch * scale_post * post_gain[...]
    squares = row_sum(jnp.sum(resid * resid, axis=1, keepdims=True), slots_two, ts, tr, nw)
    scale_final = lax.rsqrt(squares / model + EPS)
    final[v] = (resid * scale_final * final_gain[...]).astype(BF16)
    branch_out[...] = branch
    resid_out[...] = resid
    scales[0] = jnp.broadcast_to(scale_post, scales.shape[1:])
    scales[1] = jnp.broadcast_to(scale_final, scales.shape[1:])
    gather_rows(final, gs, gr, hs, hr, nv)


def head_kernel(
    nv, nw,
    logits, ids, weights,
    delta, loss,
    mine, land, col_slots, row_slots, capped,
    xs, xr, cs, cr, rs, rr, ds, dr,
):
    v, w = place()
    sub, tokens = logits.shape[1:]
    column = [(lax.rem(v + k, nv), w) for k in range(1, nv)]
    row = row_peers(nw)
    greet(column + row)
    copies = []
    for k in range(1, nw):
        peer = lax.rem(w + k, nw)
        mine[k - 1] = logits[peer].astype(BF16)
        copy = remote(mine.at[k - 1], land.at[k - 1], xs.at[k], xr.at[k], (v, peer))
        copy.start()
        copies.append(copy)
    for copy in copies:
        copy.wait()
    total = logits[w]
    for k in range(nw - 1):
        total = total + land[k].astype(F32)
    cap = CAP * jnp.tanh(total / CAP)
    capped[...] = cap
    first = (v * nw + w) * sub
    hits = (lax.broadcasted_iota(jnp.int32, (sub, tokens), 0) + first) == ids[...]
    sums = jnp.sum(jnp.exp(cap - CAP), axis=0, keepdims=True)
    marks = jnp.sum(jnp.where(hits, cap, 0.0), axis=0, keepdims=True)
    which = lax.broadcasted_iota(jnp.int32, (8, tokens), 0)
    col_slots[v] = jnp.where(which == 0, sums, jnp.where(which == 1, marks, 0.0))
    copies = []
    for k in range(1, nv):
        copy = remote(col_slots.at[v], col_slots.at[v], cs.at[k], cr.at[k], column[k - 1])
        copy.start()
        copies.append(copy)
    for copy in copies:
        copy.wait()
    row_slots[w] = jnp.sum(col_slots[...], axis=0)
    copies = []
    for k in range(1, nw):
        copy = remote(row_slots.at[w], row_slots.at[w], rs.at[k], rr.at[k], row[k - 1])
        copy.start()
        copies.append(copy)
    for copy in copies:
        copy.wait()
    both = jnp.sum(row_slots[...], axis=0)
    lognorm = CAP + jnp.log(both[0:1])
    weight = weights[...]
    logprob = both[1:2] - lognorm
    mean = -jnp.sum(weight * logprob, axis=1, keepdims=True) / tokens
    loss[...] = jnp.broadcast_to(mean, loss.shape)
    cap = capped[...]
    prob = jnp.exp(cap - lognorm)
    slope = 1.0 - (cap / CAP) ** 2
    delta[w] = (-weight * (jnp.where(hits, 1.0, 0.0) - prob) * slope).astype(BF16)
    copies = []
    for k in range(1, nw):
        copy = remote(delta.at[w], delta.at[w], ds.at[k], dr.at[k], row[k - 1])
        copy.start()
        copies.append(copy)
    for copy in copies:
        copy.wait()


def turn_kernel(
    nv, nw, model,
    part, branch_ref, resid_ref, scales, post_gain, final_gain,
    grad_branch, grad_resid_out,
    paired, stage, land, slots, slots_two,
    ss, sr, ts, tr, gs, gr, hs, hr, ps, pr, qs, qr,
):
    v, _ = place()
    greet(column_peers(nv) + row_peers(nw))
    grad_final = scatter_sum(part, paired, stage, land, ps, pr, qs, qr, nv)
    resid, branch = resid_ref[...], branch_ref[...]
    scale_post, scale_final = scales[0][:, :1], scales[1][:, :1]
    weighted = grad_final * final_gain[...]
    back = row_sum(jnp.sum(weighted * resid, axis=1, keepdims=True), slots, ss, sr, nw)
    grad_resid = scale_final * weighted - resid * (
        scale_final * scale_final * scale_final * back / model
    )
    weighted = grad_resid * post_gain[...]
    back = row_sum(jnp.sum(weighted * branch, axis=1, keepdims=True), slots_two, ts, tr, nw)
    grad_branch[v] = (
        scale_post * weighted - branch * (scale_post * scale_post * scale_post * back / model)
    ).astype(BF16)
    grad_resid_out[...] = grad_resid
    gather_rows(grad_branch, gs, gr, hs, hr, nv)


def active_kernel(nw, part, value, slope, gate_in, up_in, mine, land, send, recv):
    v, w = place()
    greet(row_peers(nw))
    mine[...] = part[...].astype(BF16)
    copies = []
    for k in range(1, nw):
        copy = remote(mine, land.at[k - 1], send.at[k], recv.at[k], (v, lax.rem(w + k, nw)))
        copy.start()
        copies.append(copy)
    for copy in copies:
        copy.wait()
    total = part[...]
    for k in range(nw - 1):
        total = total + land[k].astype(F32)
    gate_in[...] = (total * slope[...]).astype(BF16)
    up_in[...] = (total * value[...]).astype(BF16)


def tail_kernel(
    nv, nw, model,
    part, hidden, pre_gain, scale, grad_resid,
    out,
    paired, stage, land, slots,
    ss, sr, ps, pr, qs, qr,
):
    greet(column_peers(nv) + row_peers(nw))
    grad_normed = scatter_sum(part, paired, stage, land, ps, pr, qs, qr, nv)
    inputs = hidden[...].astype(F32)
    factor = scale[...][:, :1]
    weighted = grad_normed * pre_gain[...]
    back = row_sum(jnp.sum(weighted * inputs, axis=1, keepdims=True), slots, ss, sr, nw)
    out[...] = (
        grad_resid[...]
        + factor * weighted
        - inputs * (factor * factor * factor * back / model)
    ).astype(BF16)


def call(kernel, number, outs, scratch, name):
    vmem = pl.BlockSpec(memory_space=pltpu.VMEM)

    def run(*operands):
        return pl.pallas_call(
            kernel,
            out_shape=tuple(jax.ShapeDtypeStruct(shape, kind) for shape, kind in outs),
            in_specs=[vmem] * len(operands),
            out_specs=tuple(vmem for _ in outs),
            scratch_shapes=scratch,
            compiler_params=pltpu.CompilerParams(
                collective_id=number, has_side_effects=True, vmem_limit_bytes=LIMIT
            ),
            name=name,
        )(*operands)

    return run


def shards(
    hidden,
    pre_gain,
    post_gain,
    final_gain,
    gate_weight,
    up_weight,
    down_weight,
    head_weight,
    token_ids,
    rewards,
):
    nv, nw = lax.axis_size("vocab"), lax.axis_size("width")
    own, wide = hidden.shape
    model = wide * nw
    tokens = nv * own
    chips = nv // 2
    units = gate_weight.shape[1]
    vocab_dev = head_weight.shape[1]
    sub = vocab_dev // nw
    pre_gain, post_gain, final_gain = (g[None, :] for g in (pre_gain, post_gain, final_gain))

    sums = pltpu.VMEM((nw, own, 128), F32)
    row_sems = [DMA((nw,)), DMA((nw,))]
    chip_sems = [DMA((chips,)), DMA((chips,))]
    block = pltpu.VMEM((chips, own, wide), BF16)
    gather_sems = chip_sems * 2

    normed, scale = call(
        functools.partial(pre_kernel, nv, nw, model),
        0,
        [((nv, own, wide), BF16), ((own, 128), F32)],
        [sums] + row_sems + gather_sems,
        "pre_norm",
    )(hidden, pre_gain)
    normed = normed.reshape(tokens, wide)
    gate_part = jnp.dot(normed, gate_weight, preferred_element_type=F32)
    up_part = jnp.dot(normed, up_weight, preferred_element_type=F32)
    active, value, slope = call(
        functools.partial(gate_kernel, nw),
        1,
        [((tokens, units), BF16), ((tokens, units), F32), ((tokens, units), F32)],
        [
            pltpu.VMEM((2, tokens, units), BF16),
            pltpu.VMEM((nw - 1, 2, tokens, units), BF16),
            DMA((nw, 2)),
            DMA((nw, 2)),
        ],
        "gate_sum",
    )(gate_part, up_part)
    branch_part = jnp.dot(active, down_weight, preferred_element_type=F32).astype(BF16)
    final, branch, resid, scales = call(
        functools.partial(post_kernel, nv, nw, model),
        2,
        [((nv, own, wide), BF16), ((own, wide), F32), ((own, wide), F32), ((2, own, 128), F32)],
        [block, block, block, sums, sums] + row_sems * 2 + gather_sems + chip_sems * 2,
        "post_norm",
    )(branch_part.reshape(chips, 2, own, wide), hidden, post_gain, final_gain)
    final = final.reshape(tokens, wide)
    logits = contract(head_weight, final, 0, 1).reshape(nw, sub, tokens)
    weights = jnp.repeat(rewards, tokens // rewards.shape[0])[None, :]
    delta, loss = call(
        functools.partial(head_kernel, nv, nw),
        3,
        [((nw, sub, tokens), BF16), ((8, 128), F32)],
        [
            pltpu.VMEM((nw - 1, sub, tokens), BF16),
            pltpu.VMEM((nw - 1, sub, tokens), BF16),
            pltpu.VMEM((nv, 8, tokens), F32),
            pltpu.VMEM((nw, 8, tokens), F32),
            pltpu.VMEM((sub, tokens), F32),
        ]
        + row_sems
        + [DMA((nv,)), DMA((nv,))]
        + row_sems * 2,
        "head_loss",
    )(logits, token_ids[None, :], weights)
    delta = delta.reshape(vocab_dev, tokens)
    final_part = contract(delta, head_weight, 0, 1).astype(BF16)
    grad_branch, grad_resid = call(
        functools.partial(turn_kernel, nv, nw, model),
        4,
        [((nv, own, wide), BF16), ((own, wide), F32)],
        [block, block, block, sums, sums] + row_sems * 2 + gather_sems + chip_sems * 2,
        "turn",
    )(final_part.reshape(chips, 2, own, wide), branch, resid, scales, post_gain, final_gain)
    grad_branch = grad_branch.reshape(tokens, wide)
    active_part = contract(grad_branch, down_weight, 1, 1)
    gate_in, up_in = call(
        functools.partial(active_kernel, nw),
        5,
        [((tokens, units), BF16), ((tokens, units), BF16)],
        [
            pltpu.VMEM((tokens, units), BF16),
            pltpu.VMEM((nw - 1, tokens, units), BF16),
        ]
        + row_sems,
        "active_sum",
    )(active_part, value, slope)
    normed_part = (
        contract(gate_in, gate_weight, 1, 1) + contract(up_in, up_weight, 1, 1)
    ).astype(BF16)
    (grad_hidden,) = call(
        functools.partial(tail_kernel, nv, nw, model),
        6,
        [((own, wide), BF16)],
        [block, block, block, sums] + row_sems + chip_sems * 2,
        "tail",
    )(normed_part.reshape(chips, 2, own, wide), hidden, pre_gain, scale, grad_resid)
    grad_head = contract(final, delta, 0, 1).astype(BF16)
    grad_down = contract(active, grad_branch, 0, 0).astype(BF16)
    grad_gate = contract(normed, gate_in, 0, 0).astype(BF16)
    grad_up = contract(normed, up_in, 0, 0).astype(BF16)
    return (grad_hidden, grad_gate, grad_up, grad_down, grad_head, loss[0, 0])


def solution(mesh):
    return jax.shard_map(
        shards,
        mesh=mesh,
        in_specs=(
            P("vocab", "width"),
            P("width"),
            P("width"),
            P("width"),
            P("width", "vocab"),
            P("width", "vocab"),
            P("vocab", "width"),
            P("width", "vocab"),
            P(),
            P(),
        ),
        out_specs=(
            P("vocab", "width"),
            P("width", "vocab"),
            P("width", "vocab"),
            P("vocab", "width"),
            P("width", "vocab"),
            P(),
        ),
        check_vma=False,
    )
```

time: 553 us -> 213 us (0.39)
  waiting for transfers between devices: 347 us -> 0 us
  Pallas kernels: 0 us -> 143 us
  blocking collectives: 94.5 us -> 0 us
  other arithmetic: 19.6 us -> 0.01 us
  between operations: 16.1 us -> 0.98 us
  matrix products: 71.4 us -> 60.8 us
  local copies, waits for them, and re-layouts: 2.15 us -> 7.98 us
    psum x4 -> x0, waiting for transfers between devices: 256 us -> none  [the longest x1 93.9 us: shards(): lax.psum(jnp.dot(active, down_weight, preferred_element_type=jnp.float32)...]
    pallas_call x0 -> x7, Pallas kernels: none -> 143 us  [run(): pl.pallas_call(kernel, out_shape=tuple((jax.ShapeDtypeStruct(shape, kind)...]
    reduce_scatter x2 -> x0, waiting for transfers between devices: 69.5 us -> none  [the longest x1 39.4 us: shards(): lax.psum_scatter(contract(grad_gate_in, gate_weight, 1, 1) + contract(gra...]
    psum x7 -> x0, blocking collectives: 69.4 us -> none  [the longest x1 39.4 us: shards(): lax.psum((jnp.sum(jnp.exp(capped - CAP), axis=0), jnp.sum(jnp.where(hits,...]
    all_gather x1 -> x0, blocking collectives: 25.1 us -> none  [shards(): gathered = lax.all_gather(hidden, 'vocab', axis=0, tiled=True)]
    all_gather x1 -> x0, waiting for transfers between devices: 22 us -> none  [shards(): piece = lax.all_gather(delta, 'width', axis=0, tiled=True)]
    reduce_sum x8 -> x0, other arithmetic: 9.68 us -> none  [the longest x1 2.7 us: shards(): jnp.sum(weighted_post * branch, axis=1)]
    convert_element_type x5 -> x0, other arithmetic: 8.8 us -> none  [the longest x1 2.58 us: shards(): (-weights[None, :] * (hits.astype(jnp.float32) - prob) * slope).astype(jn...]
  transfers between devices with their start and end apart: 7 -> 0, of which waited for: 7 -> 0; matrix products, arithmetic and copies ran while one was open for 3% -> 0% of each run, Pallas kernels for 0% -> 0%
where the time goes in v1:
time: 213 us
  Pallas kernels  143 us (67%)
  matrix products  60.8 us (29%)
  local copies, waits for them, and re-layouts  7.98 us (4%)
    pallas_call x7, Pallas kernels, run(): pl.pallas_call(kernel, out_shape=tuple((jax.ShapeDtypeStruct(shape, kind)...  143 us
    dot_general x9, matrix products, contract(): lax.dot_general(left, right, (((left_dim,), (right_dim,)), ((), ())), pre...  55.3 us

profile of v1, /device:TPU:0, one launch (start us, length us, event | category | flops | bytes accessed | tf_op | source)
XLA Modules:
  0.0 212.7 jit_solution(13852719810778424457)
XLA Ops:
  0.6 0.7 broadcast_in_dim.19
  1.4 0.1 broadcast_in_dim_reshape.3.weights
  1.4 0.7 broadcast_in_dim.15.gain.pre_gain
  2.2 0.7 broadcast_in_dim.16.post_gain
  2.9 0.7 broadcast_in_dim.17.final_gain
  3.6 0.8 copy-done.8
  4.4 15.2 %pre_norm.1 = (bf16[16,8,2304]{2,1,0:T(8,128)(2,1)S(1)}, f32[8,128]{1,0:T(8,128)S(1)}) custom-call(bf16[8,2304]{1,0:T(8,128)(2,1)S(1)} %copy-done.8, f32[1,2304]{1,0:T(1,128)S(1)} %broadcast_in_dim.15.gain.pre_gain), custom_call_target="tpu_custom_call" | custom-call | tf_op jit(solution)/shard_map/pre_norm/pallas_call | solution.py:335
  19.6 0.0 slice-start
  19.6 3.6 %fusion.8.up_part = f32[128,1152]{1,0:T(8,128)S(1)} fusion(bf16[2304,1152]{1,0:T(8,128)(2,1)} %param.15, bf16[16,8,2304]{2,1,0:T(8,128)(2,1)S(1)} %get-tuple-element.21), kind=kOutput, calls=%fused_computation.16 | convolution fusion | flops 679477248 | bytes 6488064 | tf_op jit(solution)/shard_map/dot_general | solution.py:387
  23.2 0.0 slice-start.1
  23.2 0.9 fusion.10.gate_part
  24.2 16.3 %gate_sum.1 = (bf16[128,1152]{1,0:T(8,128)(2,1)S(1)}, f32[128,1152]{1,0:T(8,128)S(1)}, f32[128,1152]{1,0:T(8,128)S(1)}) custom-call(f32[128,1152]{1,0:T(8,128)S(1)} %fusion.10.gate_part, f32[128,1152]{1,0:T(8,128)S(1)} %fusion.8.up_part), custom_call_target="tpu_custom_call" | custom-call | tf_op jit(solution)/shard_map/gate_sum/pallas_call | solution.py:335
  40.6 1.0 convolution_convert_fusion.5
  41.6 26.0 %post_norm.1 = (bf16[16,8,2304]{2,1,0:T(8,128)(2,1)S(1)}, f32[8,2304]{1,0:T(8,128)S(1)}, f32[8,2304]{1,0:T(8,128)S(1)}, f32[2,8,128]{2,1,0:T(8,128)S(1)}) custom-call(bf16[8,2,8,2304]{3,2,1,0:T(8,128)(2,1)S(1)} %bitcast.48, bf16[8,2304]{1,0:T(8,128)(2,1)S(1)} %copy-done.9, f32[1,2304]{1,0:T(1,128)S(1)} %broadcast_in_dim.16.post_gain, ...), custom_call_target="tpu_custom_call" | custom-call | tf_op jit(solution)/shard_map/post_norm/pallas_call | solution.py:335
  67.6 10.5 %convolution_bitcast_fusion = f32[4096,128]{0,1:T(8,128)} fusion(bf16[2304,4096]{1,0:T(8,128)(2,1)} %param.17, bf16[16,8,2304]{2,1,0:T(8,128)(2,1)S(1)} %get-tuple-element.23), kind=kOutput, calls=%fused_computation.4 | convolution fusion | flops 2415919104 | bytes 21561344 | tf_op jit(solution)/shard_map/dot_general | solution.py:22
  78.1 2.1 copy.17
  80.2 37.0 %head_loss.1 = (bf16[2,2048,128]{2,1,0:T(8,128)(2,1)S(1)}, f32[8,128]{1,0:T(8,128)S(1)}) custom-call(f32[2,2048,128]{2,1,0:T(8,128)S(1)} %bitcast.44, s32[1,128]{1,0:T(1,128)S(1)} %bitcast.50, f32[1,128]{1,0:T(1,128)S(1)} %broadcast_in_dim_reshape.3.weights), custom_call_target="tpu_custom_call" | custom-call | tf_op jit(solution)/shard_map/head_loss/pallas_call | solution.py:335
  117.3 1.0 copy-done
  118.2 0.5 slice.3
  118.7 13.1 %convolution_convert_fusion.4 = bf16[128,2304]{1,0:T(8,128)(2,1)S(1)} fusion(bf16[4096,128]{1,0:T(8,128)(2,1)} %bitcast.45, bf16[2304,4096]{1,0:T(8,128)(2,1)} %param.17), kind=kOutput, calls=%fused_computation.6 | convolution fusion | flops 2416214016 | bytes 20512768 | tf_op jit(solution)/shard_map/dot_general | solution.py:22
  131.9 24.6 %turn.1 = (bf16[16,8,2304]{2,1,0:T(8,128)(2,1)S(1)}, f32[8,2304]{1,0:T(8,128)S(1)}) custom-call(bf16[8,2,8,2304]{3,2,1,0:T(8,128)(2,1)S(1)} %bitcast.47, f32[8,2304]{1,0:T(8,128)S(1)} %get-tuple-element.25.branch_ref, f32[8,2304]{1,0:T(8,128)S(1)} %get-tuple-element.26.resid_ref, f32[2,8,128]{2,1,0:T(8,128)S(1)} %get-tuple-element.27.scales, ...), custom_call_target="tpu_custom_call" | custom-call | tf_op jit(solution)/shard_map/turn/pallas_call | solution.py:335
  156.5 4.4 %fusion.2.part = f32[128,1152]{1,0:T(8,128)S(1)} fusion(bf16[1152,2304]{1,0:T(8,128)(2,1)} %param.16, bf16[16,8,2304]{2,1,0:T(8,128)(2,1)S(1)} %get-tuple-element.28), kind=kOutput, calls=%fused_computation.10 | convolution fusion | flops 679477248 | bytes 6488064 | tf_op jit(solution)/shard_map/dot_general | solution.py:22
  161.0 0.0 slice-start.3
  161.0 9.6 %active_sum.1 = (bf16[128,1152]{1,0:T(8,128)(2,1)S(1)}, bf16[128,1152]{1,0:T(8,128)(2,1)S(1)}) custom-call(f32[128,1152]{1,0:T(8,128)S(1)} %fusion.2.part, f32[128,1152]{1,0:T(8,128)S(1)} %copy-done.5, f32[128,1152]{1,0:T(8,128)S(1)} %copy-done.7), custom_call_target="tpu_custom_call" | custom-call | tf_op jit(solution)/shard_map/active_sum/pallas_call | solution.py:335
  170.6 4.1 %fusion.12 = f32[128,2304]{1,0:T(8,128)S(1)} fusion(bf16[128,1152]{1,0:T(8,128)(2,1)S(1)} %get-tuple-element.31, bf16[2304,1152]{1,0:T(8,128)(2,1)} %param.14), kind=kOutput, calls=%fused_computation.20 | convolution fusion | flops 679477248 | bytes 6782976 | tf_op jit(solution)/shard_map/dot_general | solution.py:22
  174.7 1.6 fusion
  176.2 14.2 %tail.1 = bf16[8,2304]{1,0:T(8,128)(2,1)S(1)} custom-call(bf16[8,2,8,2304]{3,2,1,0:T(8,128)(2,1)S(1)} %bitcast.49, bf16[8,2304]{1,0:T(8,128)(2,1)S(1)} %copy-done.9, f32[1,2304]{1,0:T(1,128)S(1)} %broadcast_in_dim.15.gain.pre_gain, f32[8,128]{1,0:T(8,128)S(1)} %get-tuple-element.33.scale, f32[8,2304]{1,0:T(8,128)S(1)} %get-tuple-element.34.grad_resid), custom_call_target="tpu_custom_call" | custom-call | tf_op jit(solution)/shard_map/tail/pallas_call | solution.py:335
  190.5 4.0 %convolution_convert_fusion.1 = bf16[1152,2304]{1,0:T(8,128)(2,1)} fusion(bf16[128,1152]{1,0:T(8,128)(2,1)S(1)} %copy-done.3, bf16[16,8,2304]{2,1,0:T(8,128)(2,1)S(1)} %get-tuple-element.28), kind=kOutput, calls=%fused_computation.1 | convolution fusion | flops 682131456 | bytes 6193152 | tf_op jit(solution)/shard_map/dot_general | solution.py:22
  194.4 4.2 %convolution_convert_fusion.2 = bf16[2304,1152]{1,0:T(8,128)(2,1)} fusion(bf16[128,1152]{1,0:T(8,128)(2,1)S(1)} %get-tuple-element.32, bf16[16,8,2304]{2,1,0:T(8,128)(2,1)S(1)} %get-tuple-element.21), kind=kOutput, calls=%fused_computation.2 | convolution fusion | flops 682131456 | bytes 6193152 | tf_op jit(solution)/shard_map/dot_general | solution.py:22
  198.6 4.0 %convolution_convert_fusion.3 = bf16[2304,1152]{1,0:T(8,128)(2,1)} fusion(bf16[128,1152]{1,0:T(8,128)(2,1)S(1)} %get-tuple-element.31, bf16[16,8,2304]{2,1,0:T(8,128)(2,1)S(1)} %get-tuple-element.21), kind=kOutput, calls=%fused_computation.3 | convolution fusion | flops 682131456 | bytes 6193152 | tf_op jit(solution)/shard_map/dot_general | solution.py:22
  202.6 9.5 %convolution_convert_fusion = bf16[2304,4096]{1,0:T(8,128)(2,1)} fusion(bf16[4096,128]{1,0:T(8,128)(2,1)S(1)} %bitcast.46, bf16[16,8,2304]{2,1,0:T(8,128)(2,1)S(1)} %get-tuple-element.23), kind=kOutput, calls=%fused_computation | convolution fusion | flops 2425356288 | bytes 20512768 | tf_op jit(solution)/shard_map/dot_general | solution.py:22
  212.1 0.6 copy.19
  (29 shorter events, 0.1 us)
Async XLA Ops:
  3.6 0.8 copy-start.8
  4.4 18.9 %copy-start.11 = (bf16[2304,1152]{1,0:T(8,128)(2,1)S(1)}, bf16[2304,1152]{1,0:T(8,128)(2,1)}, u32[]{:S(2)}) copy-start(bf16[2304,1152]{1,0:T(8,128)(2,1)} %param.14) | copy-start | bytes 15925252
  19.6 20.9 %slice-start = ((s8[5308416]{0:T(1024)(128)(4,1)}), s8[4194304]{0:T(1024)(128)(4,1)S(1)}, s32[]{:S(2)}) async-start(s8[5308416]{0:T(1024)(128)(4,1)} %bitcast.51), calls=%async_computation | async-start | bytes 8388608
  23.2 17.3 %slice-start.1 = ((s8[5308416]{0:T(1024)(128)(4,1)}), s8[1114112]{0:T(1024)(128)(4,1)S(1)}, s32[]{:S(2)}) async-start(s8[5308416]{0:T(1024)(128)(4,1)} %bitcast.51), calls=%async_computation.1 | async-start | bytes 2228224
  24.2 17.4 %copy-start.9 = (bf16[8,2304]{1,0:T(8,128)(2,1)S(1)}, bf16[8,2304]{1,0:T(8,128)(2,1)}, u32[]{:S(2)}) copy-start(bf16[8,2304]{1,0:T(8,128)(2,1)} %hidden.5) | copy-start | bytes 110596
  40.5 1.0 copy-start.2
  40.5 27.1 %copy-start.4 = (f32[128,1152]{1,0:T(8,128)}, f32[128,1152]{1,0:T(8,128)S(1)}, u32[]{:S(2)}) copy-start(f32[128,1152]{1,0:T(8,128)S(1)} %get-tuple-element.29.value) | copy-start | bytes 1769476
  40.5 27.1 %copy-start.6 = (f32[128,1152]{1,0:T(8,128)}, f32[128,1152]{1,0:T(8,128)S(1)}, u32[]{:S(2)}) copy-start(f32[128,1152]{1,0:T(8,128)S(1)} %get-tuple-element.30.slope) | copy-start | bytes 1769476
  67.6 12.6 %copy-start.10 = (s32[128]{0:T(128)S(1)}, s32[128]{0:T(128)}, u32[]{:S(2)}) copy-start(s32[128]{0:T(128)} %param.18) | copy-start | bytes 1540
  117.2 1.0 copy-start
  131.9 29.1 %copy-start.5 = (f32[128,1152]{1,0:T(8,128)S(1)}, f32[128,1152]{1,0:T(8,128)}, u32[]{:S(2)}) copy-start(f32[128,1152]{1,0:T(8,128)} %copy-done.4) | copy-start | bytes 1769476
  131.9 29.1 %copy-start.7 = (f32[128,1152]{1,0:T(8,128)S(1)}, f32[128,1152]{1,0:T(8,128)}, u32[]{:S(2)}) copy-start(f32[128,1152]{1,0:T(8,128)} %copy-done.6) | copy-start | bytes 1769476
  156.5 18.1 %slice-start.2 = ((s8[5308416]{0:T(1024)(128)(4,1)}), s8[4194304]{0:T(1024)(128)(4,1)S(1)}, s32[]{:S(2)}) async-start(s8[5308416]{0:T(1024)(128)(4,1)} %bitcast.53), calls=%async_computation.2 | async-start | bytes 8388608
  161.0 13.7 %slice-start.3 = ((s8[5308416]{0:T(1024)(128)(4,1)}), s8[1114112]{0:T(1024)(128)(4,1)S(1)}, s32[]{:S(2)}) async-start(s8[5308416]{0:T(1024)(128)(4,1)} %bitcast.53), calls=%async_computation.3 | async-start | bytes 2228224
  174.7 15.8 %copy-start.3 = (bf16[128,1152]{1,0:T(8,128)(2,1)S(1)}, bf16[128,1152]{1,0:T(8,128)(2,1)}, u32[]{:S(2)}) copy-start(bf16[128,1152]{1,0:T(8,128)(2,1)} %copy-done.2) | copy-start | bytes 884740
  198.6 4.0 %copy-start.1 = (bf16[2,2048,128]{2,1,0:T(8,128)(2,1)S(1)}, bf16[2,2048,128]{2,1,0:T(8,128)(2,1)}, u32[]{:S(2)}) copy-start(bf16[2,2048,128]{2,1,0:T(8,128)(2,1)} %copy-done) | copy-start | bytes 3145732

commit v2 on v1

--- a/solution.py
+++ b/solution.py
@@ -132,14 +132,14 @@
     return total
 
 
-def pre_kernel(nv, nw, model, hidden, gain, normed, scale, slots, ss, sr, gs, gr, hs, hr):
+def pre_kernel(nv, nw, model, hidden, gains, normed, scale, slots, ss, sr, gs, gr, hs, hr):
     v, _ = place()
     greet(column_peers(nv) + row_peers(nw))
     inputs = hidden[...].astype(F32)
     squares = row_sum(jnp.sum(inputs * inputs, axis=1, keepdims=True), slots, ss, sr, nw)
     factor = lax.rsqrt(squares / model + EPS)
     scale[...] = jnp.broadcast_to(factor, scale.shape)
-    normed[v] = (inputs * factor * gain[...]).astype(BF16)
+    normed[v] = (inputs * factor * gains[0:1]).astype(BF16)
     gather_rows(normed, gs, gr, hs, hr, nv)
 
 
@@ -177,7 +177,7 @@
 
 def post_kernel(
     nv, nw, model,
-    part, hidden, post_gain, final_gain,
+    part, hidden, gains,
     final, branch_out, resid_out, scales,
     paired, stage, land, slots, slots_two,
     ss, sr, ts, tr, gs, gr, hs, hr, ps, pr, qs, qr,
@@ -187,10 +187,10 @@
     branch = scatter_sum(part, paired, stage, land, ps, pr, qs, qr, nv)
     squares = row_sum(jnp.sum(branch * branch, axis=1, keepdims=True), slots, ss, sr, nw)
     scale_post = lax.rsqrt(squares / model + EPS)
-    resid = hidden[...].astype(F32) + branch * scale_post * post_gain[...]
+    resid = hidden[...].astype(F32) + branch * scale_post * gains[1:2]
     squares = row_sum(jnp.sum(resid * resid, axis=1, keepdims=True), slots_two, ts, tr, nw)
     scale_final = lax.rsqrt(squares / model + EPS)
-    final[v] = (resid * scale_final * final_gain[...]).astype(BF16)
+    final[v] = (resid * scale_final * gains[2:3]).astype(BF16)
     branch_out[...] = branch
     resid_out[...] = resid
     scales[0] = jnp.broadcast_to(scale_post, scales.shape[1:])
@@ -200,36 +200,59 @@
 
 def head_kernel(
     nv, nw,
-    logits, ids, weights,
-    delta, loss,
-    mine, land, col_slots, row_slots, capped,
-    xs, xr, cs, cr, rs, rr, ds, dr,
+    final, head, ids, weights,
+    delta, loss, part,
+    held, mine, land, col_slots, row_slots, capped, total,
+    ls, xs, xr, cs, cr, rs, rr, ds, dr,
 ):
     v, w = place()
-    sub, tokens = logits.shape[1:]
+    chunks, tokens, width = capped.shape
+    sub = chunks * width
+
+    def columns(peer, j):
+        return pl.ds(pl.multiple_of(peer * sub + j * width, 128), width)
+
+    loads = {}
+    for k in list(range(1, nw)) + [0]:
+        for j in range(chunks):
+            where = columns(lax.rem(w + k, nw), j)
+            loads[k, j] = pltpu.make_async_copy(head.at[:, where], held.at[:, where], ls.at[k, j])
+            loads[k, j].start()
     column = [(lax.rem(v + k, nv), w) for k in range(1, nv)]
     row = row_peers(nw)
     greet(column + row)
-    copies = []
+    sent = {}
     for k in range(1, nw):
         peer = lax.rem(w + k, nw)
-        mine[k - 1] = logits[peer].astype(BF16)
-        copy = remote(mine.at[k - 1], land.at[k - 1], xs.at[k], xr.at[k], (v, peer))
-        copy.start()
-        copies.append(copy)
-    for copy in copies:
-        copy.wait()
-    total = logits[w]
-    for k in range(nw - 1):
-        total = total + land[k].astype(F32)
-    cap = CAP * jnp.tanh(total / CAP)
-    capped[...] = cap
+        for j in range(chunks):
+            loads[k, j].wait()
+            mine[k - 1, j] = jnp.dot(
+                final[...], held[:, columns(peer, j)], preferred_element_type=F32
+            ).astype(BF16)
+            sent[k, j] = remote(
+                mine.at[k - 1, j], land.at[k - 1, j], xs.at[k, j], xr.at[k, j], (v, peer)
+            )
+            sent[k, j].start()
+    for j in range(chunks):
+        loads[0, j].wait()
+        capped[j] = jnp.dot(final[...], held[:, columns(w, j)], preferred_element_type=F32)
     first = (v * nw + w) * sub
-    hits = (lax.broadcasted_iota(jnp.int32, (sub, tokens), 0) + first) == ids[...]
-    sums = jnp.sum(jnp.exp(cap - CAP), axis=0, keepdims=True)
-    marks = jnp.sum(jnp.where(hits, cap, 0.0), axis=0, keepdims=True)
-    which = lax.broadcasted_iota(jnp.int32, (8, tokens), 0)
-    col_slots[v] = jnp.where(which == 0, sums, jnp.where(which == 1, marks, 0.0))
+    lanes = lax.broadcasted_iota(jnp.int32, (tokens, width), 1)
+    sums = jnp.zeros((tokens, 1), F32)
+    marks = jnp.zeros((tokens, 1), F32)
+    for j in range(chunks):
+        logits = capped[j]
+        for k in range(1, nw):
+            sent[k, j].wait()
+            logits = logits + land[k - 1, j].astype(F32)
+        cap = CAP * jnp.tanh(logits / CAP)
+        capped[j] = cap
+        hits = lanes + (first + j * width) == ids[...]
+        sums = sums + jnp.sum(jnp.exp(cap - CAP), axis=1, keepdims=True)
+        marks = marks + jnp.sum(jnp.where(hits, cap, 0.0), axis=1, keepdims=True)
+    which = lax.broadcasted_iota(jnp.int32, (tokens, 128), 1)
+    both = jnp.where(which == 0, sums, jnp.where(which == 1, marks, 0.0))
+    col_slots[v] = jnp.transpose(both)[:8]
     copies = []
     for k in range(1, nv):
         copy = remote(col_slots.at[v], col_slots.at[v], cs.at[k], cr.at[k], column[k - 1])
@@ -246,27 +269,47 @@
     for copy in copies:
         copy.wait()
     both = jnp.sum(row_slots[...], axis=0)
-    lognorm = CAP + jnp.log(both[0:1])
+    both = jnp.transpose(jnp.concatenate([both] * 16, axis=0))
+    lognorm = CAP + jnp.log(both[:, 0:1])
     weight = weights[...]
-    logprob = both[1:2] - lognorm
-    mean = -jnp.sum(weight * logprob, axis=1, keepdims=True) / tokens
+    logprob = both[:, 1:2] - lognorm
+    mean = -jnp.sum(weight * logprob, axis=0, keepdims=True) / tokens
     loss[...] = jnp.broadcast_to(mean, loss.shape)
-    cap = capped[...]
-    prob = jnp.exp(cap - lognorm)
-    slope = 1.0 - (cap / CAP) ** 2
-    delta[w] = (-weight * (jnp.where(hits, 1.0, 0.0) - prob) * slope).astype(BF16)
-    copies = []
-    for k in range(1, nw):
-        copy = remote(delta.at[w], delta.at[w], ds.at[k], dr.at[k], row[k - 1])
-        copy.start()
-        copies.append(copy)
-    for copy in copies:
-        copy.wait()
+    sent = {}
+    for j in range(chunks):
+        cap = capped[j]
+        hits = lanes + (first + j * width) == ids[...]
+        prob = jnp.exp(cap - lognorm)
+        slope = 1.0 - (cap / CAP) ** 2
+        where = columns(w, j)
+        delta[:, where] = (-weight * (jnp.where(hits, 1.0, 0.0) - prob) * slope).astype(BF16)
+        for k in range(1, nw):
+            sent[k, j] = remote(
+                delta.at[:, where], delta.at[:, where], ds.at[k, j], dr.at[k, j], row[k - 1]
+            )
+            sent[k, j].start()
+    for k in range(nw):
+        source = lax.rem(w + nw - k, nw)
+        for j in range(chunks):
+            where = columns(source, j)
+            if k:
+                remote(
+                    delta.at[:, where], delta.at[:, where], ds.at[k, j], dr.at[k, j], row[k - 1]
+                ).wait_recv()
+            rows = contract(delta[:, where], held[:, where], 1, 1)
+            if k == 0 and j == 0:
+                total[...] = rows
+            elif k == nw - 1 and j == chunks - 1:
+                part[...] = (total[...] + rows).astype(BF16)
+            else:
+                total[...] += rows
+    for copy in sent.values():
+        copy.wait_send()
 
 
 def turn_kernel(
     nv, nw, model,
-    part, branch_ref, resid_ref, scales, post_gain, final_gain,
+    part, branch_ref, resid_ref, scales, gains,
     grad_branch, grad_resid_out,
     paired, stage, land, slots, slots_two,
     ss, sr, ts, tr, gs, gr, hs, hr, ps, pr, qs, qr,
@@ -276,12 +319,12 @@
     grad_final = scatter_sum(part, paired, stage, land, ps, pr, qs, qr, nv)
     resid, branch = resid_ref[...], branch_ref[...]
     scale_post, scale_final = scales[0][:, :1], scales[1][:, :1]
-    weighted = grad_final * final_gain[...]
+    weighted = grad_final * gains[2:3]
     back = row_sum(jnp.sum(weighted * resid, axis=1, keepdims=True), slots, ss, sr, nw)
     grad_resid = scale_final * weighted - resid * (
         scale_final * scale_final * scale_final * back / model
     )
-    weighted = grad_resid * post_gain[...]
+    weighted = grad_resid * gains[1:2]
     back = row_sum(jnp.sum(weighted * branch, axis=1, keepdims=True), slots_two, ts, tr, nw)
     grad_branch[v] = (
         scale_post * weighted - branch * (scale_post * scale_post * scale_post * back / model)
@@ -310,7 +353,7 @@
 
 def tail_kernel(
     nv, nw, model,
-    part, hidden, pre_gain, scale, grad_resid,
+    part, hidden, gains, scale, grad_resid,
     out,
     paired, stage, land, slots,
     ss, sr, ps, pr, qs, qr,
@@ -319,7 +362,7 @@
     grad_normed = scatter_sum(part, paired, stage, land, ps, pr, qs, qr, nv)
     inputs = hidden[...].astype(F32)
     factor = scale[...][:, :1]
-    weighted = grad_normed * pre_gain[...]
+    weighted = grad_normed * gains[0:1]
     back = row_sum(jnp.sum(weighted * inputs, axis=1, keepdims=True), slots, ss, sr, nw)
     out[...] = (
         grad_resid[...]
@@ -328,14 +371,17 @@
     ).astype(BF16)
 
 
-def call(kernel, number, outs, scratch, name):
+def call(kernel, number, outs, scratch, name, whole=()):
     vmem = pl.BlockSpec(memory_space=pltpu.VMEM)
 
     def run(*operands):
         return pl.pallas_call(
             kernel,
             out_shape=tuple(jax.ShapeDtypeStruct(shape, kind) for shape, kind in outs),
-            in_specs=[vmem] * len(operands),
+            in_specs=[
+                pl.BlockSpec(memory_space=pl.ANY) if i in whole else vmem
+                for i in range(len(operands))
+            ],
             out_specs=tuple(vmem for _ in outs),
             scratch_shapes=scratch,
             compiler_params=pltpu.CompilerParams(
@@ -367,7 +413,7 @@
     units = gate_weight.shape[1]
     vocab_dev = head_weight.shape[1]
     sub = vocab_dev // nw
-    pre_gain, post_gain, final_gain = (g[None, :] for g in (pre_gain, post_gain, final_gain))
+    gains = jnp.stack([pre_gain, post_gain, final_gain])
 
     sums = pltpu.VMEM((nw, own, 128), F32)
     row_sems = [DMA((nw,)), DMA((nw,))]
@@ -381,7 +427,7 @@
         [((nv, own, wide), BF16), ((own, 128), F32)],
         [sums] + row_sems + gather_sems,
         "pre_norm",
-    )(hidden, pre_gain)
+    )(hidden, gains)
     normed = normed.reshape(tokens, wide)
     gate_part = jnp.dot(normed, gate_weight, preferred_element_type=F32)
     up_part = jnp.dot(normed, up_weight, preferred_element_type=F32)
@@ -404,35 +450,40 @@
         [((nv, own, wide), BF16), ((own, wide), F32), ((own, wide), F32), ((2, own, 128), F32)],
         [block, block, block, sums, sums] + row_sems * 2 + gather_sems + chip_sems * 2,
         "post_norm",
-    )(branch_part.reshape(chips, 2, own, wide), hidden, post_gain, final_gain)
+    )(branch_part.reshape(chips, 2, own, wide), hidden, gains)
     final = final.reshape(tokens, wide)
-    logits = contract(head_weight, final, 0, 1).reshape(nw, sub, tokens)
-    weights = jnp.repeat(rewards, tokens // rewards.shape[0])[None, :]
-    delta, loss = call(
+    weights = jnp.repeat(rewards, tokens // rewards.shape[0])[:, None]
+    width = min(512, sub)
+    chunks = sub // width
+    sems = [DMA((nw, chunks)), DMA((nw, chunks))]
+    delta, loss, final_part = call(
         functools.partial(head_kernel, nv, nw),
         3,
-        [((nw, sub, tokens), BF16), ((8, 128), F32)],
+        [((tokens, vocab_dev), BF16), ((8, 128), F32), ((tokens, wide), BF16)],
         [
-            pltpu.VMEM((nw - 1, sub, tokens), BF16),
-            pltpu.VMEM((nw - 1, sub, tokens), BF16),
+            pltpu.VMEM((wide, vocab_dev), BF16),
+            pltpu.VMEM((nw - 1, chunks, tokens, width), BF16),
+            pltpu.VMEM((nw - 1, chunks, tokens, width), BF16),
             pltpu.VMEM((nv, 8, tokens), F32),
             pltpu.VMEM((nw, 8, tokens), F32),
-            pltpu.VMEM((sub, tokens), F32),
+            pltpu.VMEM((chunks, tokens, width), F32),
+            pltpu.VMEM((tokens, wide), F32),
+            DMA((nw, chunks)),
         ]
+        + sems
+        + [DMA((nv,)), DMA((nv,))]
         + row_sems
-        + [DMA((nv,)), DMA((nv,))]
-        + row_sems * 2,
+        + sems,
         "head_loss",
-    )(logits, token_ids[None, :], weights)
-    delta = delta.reshape(vocab_dev, tokens)
-    final_part = contract(delta, head_weight, 0, 1).astype(BF16)
+        whole=(1,),
+    )(final, head_weight, token_ids[:, None], weights)
     grad_branch, grad_resid = call(
         functools.partial(turn_kernel, nv, nw, model),
         4,
         [((nv, own, wide), BF16), ((own, wide), F32)],
         [block, block, block, sums, sums] + row_sems * 2 + gather_sems + chip_sems * 2,
         "turn",
-    )(final_part.reshape(chips, 2, own, wide), branch, resid, scales, post_gain, final_gain)
+    )(final_part.reshape(chips, 2, own, wide), branch, resid, scales, gains)
     grad_branch = grad_branch.reshape(tokens, wide)
     active_part = contract(grad_branch, down_weight, 1, 1)
     gate_in, up_in = call(
@@ -455,8 +506,8 @@
         [((own, wide), BF16)],
         [block, block, block, sums] + row_sems + chip_sems * 2,
         "tail",
-    )(normed_part.reshape(chips, 2, own, wide), hidden, pre_gain, scale, grad_resid)
-    grad_head = contract(final, delta, 0, 1).astype(BF16)
+    )(normed_part.reshape(chips, 2, own, wide), hidden, gains, scale, grad_resid)
+    grad_head = contract(final, delta, 0, 0).astype(BF16)
     grad_down = contract(active, grad_branch, 0, 0).astype(BF16)
     grad_gate = contract(normed, gate_in, 0, 0).astype(BF16)
     grad_up = contract(normed, up_in, 0, 0).astype(BF16)

time: 213 us -> 185 us (0.87)
  matrix products: 60.8 us -> 34.3 us
  local copies, waits for them, and re-layouts: 7.98 us -> 5.64 us
    dot_general x9 -> x7, matrix products: 55.3 us -> 28.8 us  [contract(): lax.dot_general(left, right, (((left_dim,), (right_dim,)), ((), ())), pre...]
where the time goes in v2:
time: 185 us
  Pallas kernels  144 us (78%)
  matrix products  34.3 us (19%)
  local copies, waits for them, and re-layouts  5.64 us (3%)
    pallas_call x7, Pallas kernels, run(): pl.pallas_call(kernel, out_shape=tuple((jax.ShapeDtypeStruct(shape, kind)...  144 us
    dot_general x7, matrix products, contract(): lax.dot_general(left, right, (((left_dim,), (right_dim,)), ((), ())), pre...  28.8 us

profile of v2, /device:TPU:0, one launch (start us, length us, event | category | flops | bytes accessed | tf_op | source)
XLA Modules:
  0.0 184.7 jit_solution(12649046718875256828)
XLA Ops:
  0.6 0.7 broadcast_in_dim.7
  1.4 0.7 stack.12
  2.1 0.7 stack.13
  2.8 0.7 stack.14
  3.5 0.1 broadcast_in_dim_reshape.4.weights
  3.6 0.8 copy.18.ids
  4.4 0.8 copy-done
  5.1 15.2 %pre_norm.1 = (bf16[16,8,2304]{2,1,0:T(8,128)(2,1)S(1)}, f32[8,128]{1,0:T(8,128)S(1)}) custom-call(bf16[8,2304]{1,0:T(8,128)(2,1)S(1)} %copy-done, f32[3,2304]{1,0:T(4,128)S(1)} %pad_maximum_fusion.gains), custom_call_target="tpu_custom_call" | custom-call | tf_op jit(solution)/shard_map/pre_norm/pallas_call | solution.py:378
  20.4 0.0 slice-start
  20.4 3.6 %fusion.6.up_part = f32[128,1152]{1,0:T(8,128)S(1)} fusion(bf16[2304,1152]{1,0:T(8,128)(2,1)} %param.15, bf16[16,8,2304]{2,1,0:T(8,128)(2,1)S(1)} %get-tuple-element.22), kind=kOutput, calls=%fused_computation.12 | convolution fusion | flops 679477248 | bytes 6488064 | tf_op jit(solution)/shard_map/dot_general | solution.py:433
  24.0 0.0 copy-done.2
  24.0 0.0 slice-start.1
  24.0 0.9 fusion.8.gate_part
  25.0 0.0 copy-start.1
  25.0 16.3 %gate_sum.1 = (bf16[128,1152]{1,0:T(8,128)(2,1)S(1)}, f32[128,1152]{1,0:T(8,128)S(1)}, f32[128,1152]{1,0:T(8,128)S(1)}) custom-call(f32[128,1152]{1,0:T(8,128)S(1)} %fusion.8.gate_part, f32[128,1152]{1,0:T(8,128)S(1)} %fusion.6.up_part), custom_call_target="tpu_custom_call" | custom-call | tf_op jit(solution)/shard_map/gate_sum/pallas_call | solution.py:378
  41.4 1.0 convolution_convert_fusion.4
  42.3 26.0 %post_norm.1 = (bf16[16,8,2304]{2,1,0:T(8,128)(2,1)S(1)}, f32[8,2304]{1,0:T(8,128)S(1)}, f32[8,2304]{1,0:T(8,128)S(1)}, f32[2,8,128]{2,1,0:T(8,128)S(1)}) custom-call(bf16[8,2,8,2304]{3,2,1,0:T(8,128)(2,1)S(1)} %bitcast.36, bf16[8,2304]{1,0:T(8,128)(2,1)S(1)} %copy-done.1, f32[3,2304]{1,0:T(4,128)S(1)} %pad_maximum_fusion.gains), custom_call_target="tpu_custom_call" | custom-call | tf_op jit(solution)/shard_map/post_norm/pallas_call | solution.py:378
  68.3 38.3 %head_loss.1 = (bf16[128,4096]{1,0:T(8,128)(2,1)S(1)}, f32[8,128]{1,0:T(8,128)S(1)}, bf16[128,2304]{1,0:T(8,128)(2,1)S(1)}) custom-call(bf16[128,2304]{1,0:T(8,128)(2,1)S(1)} %bitcast.35, bf16[2304,4096]{1,0:T(8,128)(2,1)} %head.1, s32[128,1]{1,0:T(8,128)S(1)} %copy.18.ids, f32[128,1]{1,0:T(8,128)S(1)} %broadcast_in_dim_reshape.4.weights), custom_call_target="tpu_custom_call" | custom-call | tf_op jit(solution)/shard_map/head_loss/pallas_call | solution.py:378
  106.7 0.5 slice.3
  107.2 24.2 %turn.1 = (bf16[16,8,2304]{2,1,0:T(8,128)(2,1)S(1)}, f32[8,2304]{1,0:T(8,128)S(1)}) custom-call(bf16[8,2,8,2304]{3,2,1,0:T(8,128)(2,1)S(1)} %bitcast.38, f32[8,2304]{1,0:T(8,128)S(1)} %get-tuple-element.26.branch_ref, f32[8,2304]{1,0:T(8,128)S(1)} %get-tuple-element.27.resid_ref, f32[2,8,128]{2,1,0:T(8,128)S(1)} %get-tuple-element.28.scales, ...), custom_call_target="tpu_custom_call" | custom-call | tf_op jit(solution)/shard_map/turn/pallas_call | solution.py:378
  131.4 0.0 slice-start.2
  131.4 1.8 fusion.2.part
  133.2 0.0 slice-start.3
  133.2 9.6 %active_sum.1 = (bf16[128,1152]{1,0:T(8,128)(2,1)S(1)}, bf16[128,1152]{1,0:T(8,128)(2,1)S(1)}) custom-call(f32[128,1152]{1,0:T(8,128)S(1)} %fusion.2.part, f32[128,1152]{1,0:T(8,128)S(1)} %get-tuple-element.30.value, f32[128,1152]{1,0:T(8,128)S(1)} %get-tuple-element.31.slope), custom_call_target="tpu_custom_call" | custom-call | tf_op jit(solution)/shard_map/active_sum/pallas_call | solution.py:378
  142.8 4.1 %fusion.11 = f32[128,2304]{1,0:T(8,128)S(1)} fusion(bf16[128,1152]{1,0:T(8,128)(2,1)S(1)} %get-tuple-element.32, bf16[2304,1152]{1,0:T(8,128)(2,1)} %param.14), kind=kOutput, calls=%fused_computation.18 | convolution fusion | flops 679477248 | bytes 6782976 | tf_op jit(solution)/shard_map/dot_general | solution.py:22
  146.9 1.6 fusion
  148.5 14.2 %tail.1 = bf16[8,2304]{1,0:T(8,128)(2,1)S(1)} custom-call(bf16[8,2,8,2304]{3,2,1,0:T(8,128)(2,1)S(1)} %bitcast.37, bf16[8,2304]{1,0:T(8,128)(2,1)S(1)} %copy-done.1, f32[3,2304]{1,0:T(4,128)S(1)} %pad_maximum_fusion.gains, f32[8,128]{1,0:T(8,128)S(1)} %get-tuple-element.34.scale, f32[8,2304]{1,0:T(8,128)S(1)} %get-tuple-element.35.grad_resid), custom_call_target="tpu_custom_call" | custom-call | tf_op jit(solution)/shard_map/tail/pallas_call | solution.py:378
  162.7 4.0 %convolution_convert_fusion.1 = bf16[1152,2304]{1,0:T(8,128)(2,1)} fusion(bf16[128,1152]{1,0:T(8,128)(2,1)S(1)} %get-tuple-element.23, bf16[16,8,2304]{2,1,0:T(8,128)(2,1)S(1)} %get-tuple-element.29), kind=kOutput, calls=%fused_computation.1 | convolution fusion | flops 682131456 | bytes 6193152 | tf_op jit(solution)/shard_map/dot_general | solution.py:22
  166.7 4.0 %convolution_convert_fusion.2 = bf16[2304,1152]{1,0:T(8,128)(2,1)} fusion(bf16[128,1152]{1,0:T(8,128)(2,1)S(1)} %get-tuple-element.33, bf16[16,8,2304]{2,1,0:T(8,128)(2,1)S(1)} %get-tuple-element.22), kind=kOutput, calls=%fused_computation.2 | convolution fusion | flops 682131456 | bytes 6193152 | tf_op jit(solution)/shard_map/dot_general | solution.py:22
  170.6 4.0 %convolution_convert_fusion.3 = bf16[2304,1152]{1,0:T(8,128)(2,1)} fusion(bf16[128,1152]{1,0:T(8,128)(2,1)S(1)} %get-tuple-element.32, bf16[16,8,2304]{2,1,0:T(8,128)(2,1)S(1)} %get-tuple-element.22), kind=kOutput, calls=%fused_computation.3 | convolution fusion | flops 682131456 | bytes 6193152 | tf_op jit(solution)/shard_map/dot_general | solution.py:22
  174.6 9.5 %convolution_convert_fusion = bf16[2304,4096]{1,0:T(8,128)(2,1)} fusion(bf16[128,4096]{1,0:T(8,128)(2,1)S(1)} %get-tuple-element.36, bf16[16,8,2304]{2,1,0:T(8,128)(2,1)S(1)} %get-tuple-element.24), kind=kOutput, calls=%fused_computation | convolution fusion | flops 2425356288 | bytes 20512768 | tf_op jit(solution)/shard_map/dot_general | solution.py:22
  184.1 0.6 copy.21
  (10 shorter events, 0.0 us)
Async XLA Ops:
  4.4 0.8 copy-start
  5.1 18.9 %copy-start.2 = (bf16[2304,1152]{1,0:T(8,128)(2,1)S(1)}, bf16[2304,1152]{1,0:T(8,128)(2,1)}, u32[]{:S(2)}) copy-start(bf16[2304,1152]{1,0:T(8,128)(2,1)} %param.14) | copy-start | bytes 15925252
  20.4 20.9 %slice-start = ((s8[5308416]{0:T(1024)(128)(4,1)}), s8[4194304]{0:T(1024)(128)(4,1)S(1)}, s32[]{:S(2)}) async-start(s8[5308416]{0:T(1024)(128)(4,1)} %bitcast.39), calls=%async_computation | async-start | bytes 8388608
  24.0 17.3 %slice-start.1 = ((s8[5308416]{0:T(1024)(128)(4,1)}), s8[1114112]{0:T(1024)(128)(4,1)S(1)}, s32[]{:S(2)}) async-start(s8[5308416]{0:T(1024)(128)(4,1)} %bitcast.39), calls=%async_computation.1 | async-start | bytes 2228224
  25.0 17.4 %copy-start.1 = (bf16[8,2304]{1,0:T(8,128)(2,1)S(1)}, bf16[8,2304]{1,0:T(8,128)(2,1)}, u32[]{:S(2)}) copy-start(bf16[8,2304]{1,0:T(8,128)(2,1)} %hidden.5) | copy-start | bytes 110596
  131.4 15.5 %slice-start.2 = ((s8[5308416]{0:T(1024)(128)(4,1)}), s8[4194304]{0:T(1024)(128)(4,1)S(1)}, s32[]{:S(2)}) async-start(s8[5308416]{0:T(1024)(128)(4,1)} %bitcast.41), calls=%async_computation.2 | async-start | bytes 8388608
  133.2 13.7 %slice-start.3 = ((s8[5308416]{0:T(1024)(128)(4,1)}), s8[1114112]{0:T(1024)(128)(4,1)S(1)}, s32[]{:S(2)}) async-start(s8[5308416]{0:T(1024)(128)(4,1)} %bitcast.41), calls=%async_computation.3 | async-start | bytes 2228224
